TPU v7x, 32 devices: a whole 2x2x4 slice. The times are simulated.
32 devices in a mesh: groups: 2 (over y), row: 4 (over x, core), col: 4 (over z).
Axes of the slice: x: 2, y: 2, z: 4, core: 2. Of those that a mesh axis runs over, the one named last changes fastest.
Arguments:
- basis_values: bfloat16 [4, 4, 2048, 1536], P('row', 'col'), may hold values from -6 to 6
- potential: float32 [4, 4, 2048], P('row', 'col'), may hold values from -0.125 to 0.125
- basis_blocks: int32 [4, 4, 12], P('row', 'col'), may hold values from 0 to 63, as said below
- factor: bfloat16 [16, 4, 128, 1024], P(None, 'row', None, 'col'), may hold values from -0.1875 to 0.1875
Outputs:
- hamiltonian: float32 [32, 4, 16, 4, 128, 128], P('groups', 'row', None, 'col'), parts along dimension 0
- product: float32 [32, 4, 128, 16, 4, 128], P('groups', 'row', None, None, 'col'), parts along dimension 0
There are 2 independent parts, one for each index of `groups`. A program takes and returns all parts, laid end to end along the dimension named above; an argument that names none is the same for every part. Nothing has to cross between parts.
Inputs may be any that keep to these rules, and one draw needn't show every extreme that they name: `basis_blocks`: the 12 blocks of one batch are distinct and lie within 16 consecutive blocks counted cyclically over the 64 blocks of the window; every such range starts at one common offset modulo 16, and every block of the range whose position in it is a multiple of 4 is on the list. Hence at most 16 of a batch's block pairs (I, J) share the same (I mod 4, J mod 4), and some pair of residues has exactly 16.
All inputs are finite; a program needn't handle non-finite values.
Results may differ from a plain program's by a relative error of at most 0.0048.
Values may be sent and summed in bfloat16 or wider, within the bound.
A program may use at most 128 MiB of HBM per device.

v0:
```python
import jax
import jax.numpy as jnp
from jax import lax
from jax.sharding import PartitionSpec as P

NB = 8192
WIN = 16


def from_root(value, axis, source):
    kept = jnp.where(lax.axis_index(axis) == source, value, 0).astype(value.dtype)
    return lax.psum(kept, axis)


def slot_ranks(targets, usable):
    count = targets.shape[0]
    order = jnp.arange(count)
    earlier = order[None, :] < order[:, None]
    same_target = (targets[:, None] == targets[None, :]) & usable[None, :] & earlier
    return jnp.sum(same_target.astype(jnp.int32), axis=1)


def pack_slots(slot_of_item, slot_count, items, labels):
    selector = jnp.arange(slot_count)[:, None] == slot_of_item[None, :]
    packed = jnp.dot(
        selector.astype(jnp.bfloat16), items, preferred_element_type=jnp.float32
    ).astype(jnp.bfloat16)
    slot_labels = jnp.sum(jnp.where(selector, labels[None, :] + 1, 0), axis=1) - 1
    return (packed, slot_labels)


def sum_into_tile(received, received_labels, tile_blocks):
    selector = received_labels[:, None] == jnp.arange(tile_blocks)[None, :]
    return lax.dot_general(
        selector.astype(jnp.bfloat16),
        received,
        (((0,), (0,)), ((), ())),
        preferred_element_type=jnp.float32,
    )


def local(basis_values, potential, basis_blocks, factor):
    row_count = lax.axis_size("row")
    col_count = lax.axis_size("col")
    device_count = row_count * col_count
    phi_batch = basis_values[0, 0]
    weight_batch = potential[0, 0]
    block_list = basis_blocks[0, 0]
    list_length = block_list.shape[0]
    block_size = factor.shape[2]
    block_area = block_size * block_size
    window = WIN
    total_blocks = NB // block_size
    local_rows = total_blocks // row_count
    local_cols = total_blocks // col_count
    tile_blocks = local_rows * local_cols
    weighted = (phi_batch * weight_batch[:, None]).astype(jnp.bfloat16)
    partial_sum = lax.dot_general(
        phi_batch, weighted, (((0,), (0,)), ((), ())), preferred_element_type=jnp.float32
    ).astype(jnp.bfloat16)
    pieces = partial_sum.reshape(list_length, block_size, list_length, block_size).transpose(
        0, 2, 1, 3
    )
    row_share = min(list_length, window // row_count)
    col_share = min(list_length, window // col_count)
    row_label = jnp.broadcast_to(block_list[:, None], (list_length, list_length)).reshape(-1)
    col_label = jnp.broadcast_to(block_list[None, :], (list_length, list_length)).reshape(-1)
    owner = row_label % row_count * col_count + col_label % col_count
    capacity = row_share * col_share
    usable = jnp.ones(owner.shape, bool)
    slot_of_item = owner * capacity + slot_ranks(owner, usable)
    local_label = row_label // row_count * local_cols + col_label // col_count
    packed, slot_labels = pack_slots(
        slot_of_item,
        device_count * capacity,
        pieces.reshape(list_length * list_length, block_area),
        local_label,
    )
    packed = packed.reshape(device_count, capacity, block_area)
    slot_labels = slot_labels.reshape(device_count, capacity)
    received, received_labels = (
        lax.all_to_all(packed, ("row", "col"), split_axis=0, concat_axis=0, tiled=True),
        lax.all_to_all(slot_labels, ("row", "col"), split_axis=0, concat_axis=0, tiled=True),
    )
    tile = sum_into_tile(received.reshape(-1, block_area), received_labels.reshape(-1), tile_blocks)
    tile = tile.reshape(local_rows, local_cols, block_size, block_size)
    hamiltonian = tile.reshape(local_rows, 1, local_cols, 1, block_size, block_size)
    tile_narrow = tile.astype(jnp.bfloat16)
    head_width = factor.shape[3] * col_count
    head_blocks = head_width // block_size
    gathered_rows = []
    for block_row in range(head_blocks):
        gathered_rows.append(
            from_root(tile_narrow[block_row // row_count], "row", block_row % row_count)
        )
    head_stack = jnp.stack(gathered_rows, axis=0)
    head_matrix = head_stack.transpose(0, 2, 1, 3).reshape(head_width, local_cols * block_size)
    piece = lax.all_gather(factor, "col", axis=3, tiled=True)
    width = piece.shape[3]
    product = jnp.dot(
        piece.reshape(local_rows * block_size, width),
        head_matrix,
        preferred_element_type=jnp.float32,
    )
    product = product.reshape(local_rows, 1, block_size, local_cols, 1, block_size)
    return (hamiltonian, product)


def solution(mesh):
    return jax.shard_map(
        local,
        mesh=mesh,
        in_specs=(
            P("row", "col", None, None),
            P("row", "col", None),
            P("row", "col", None),
            P(None, "row", None, "col"),
        ),
        out_specs=(
            P("groups", "row", None, "col", None, None),
            P("groups", "row", None, None, "col", None),
        ),
        check_vma=False,
    )
```

profile of v0, /device:TPU:0, one launch (start us, length us, event | category | flops | bytes accessed | tf_op | source)
XLA Modules:
  0.0 423.9 jit_solution(7756939959881441454)
XLA Ops:
  8.0 0.7 broadcast_in_dim.45
  8.7 0.1 reshape.286
  8.7 0.7 broadcast_in_dim.44
  9.5 0.1 reshape.285
  9.6 0.2 convert_reduce_fusion
  9.8 0.1 select_reduce_fusion
  9.9 0.7 sub.19
  10.6 7.4 %all-to-all-start = ((s32[16,1,16]{2,1,0:T(1,128)}), s32[16,1,16]{2,1,0:T(1,128)S(1)}, u32[]{:S(2)}, u32[]{:S(2)}) async-start(s32[16,1,16]{2,1,0:T(1,128)} %sub.19), calls=%async_computation | async-start | bytes 16384 | tf_op jit(solution)/shard_map/all_to_all | solution.py:83
  18.0 15.6 %fusion = bf16[1536,1536]{0,1:T(8,128)(2,1)} fusion(bf16[1,1,2048,1536]{3,2,1,0:T(8,128)(2,1)} %param.4, f32[2048]{0:T(1024)} %bitcast.89), kind=kOutput, calls=%fused_computation.4 | convolution fusion | flops 9675472896 | bytes 11018240 | tf_op jit(solution)/shard_map/dot_general | solution.py:58
  33.6 6.6 %copy.20 = bf16[1536,1536]{1,0:T(8,128)(2,1)} copy(bf16[1536,1536]{0,1:T(8,128)(2,1)} %fusion) | data formatting | bytes 9437184 | tf_op jit(solution)/shard_map/convert_element_type | solution.py:60
  40.2 9.4 %reshape.287 = bf16[12,128,12,128]{3,2,1,0:T(8,128)(2,1)} reshape(bf16[1536,1536]{1,0:T(8,128)(2,1)} %copy.20) | data formatting | bytes 9437184 | tf_op jit(solution)/shard_map/reshape | solution.py:61
  49.6 4.1 copy.21
  53.8 7.4 %convolution_convert_fusion = bf16[256,16384]{1,0:T(8,128)(2,1)} fusion(bf16[18,8,128,128]{3,2,1,0:T(8,128)(2,1)S(1)} %bitcast.76, s32[144]{0:T(256)S(1)} %multiply_add_fusion), kind=kOutput, calls=%fused_computation | convolution fusion | flops 1212190720 | bytes 13107776 | tf_op jit(solution)/shard_map/dot_general | solution.py:25
  61.2 0.0 all-to-all-done
  61.2 6.1 %all-to-all-start.1 = ((bf16[16,16,16384]{2,1,0:T(8,128)(2,1)}), bf16[16,16,16384]{2,1,0:T(8,128)(2,1)}, u32[]{:S(2)}, u32[]{:S(2)}) async-start(bf16[16,16,16384]{2,1,0:T(8,128)(2,1)} %bitcast.74), calls=%async_computation.1 | async-start | bytes 16777216 | tf_op jit(solution)/shard_map/all_to_all | solution.py:82
  67.3 0.2 all-reduce.3.cloned.1.call-start
  67.5 0.5 broadcast.328
  68.0 0.7 reduce.3
  68.7 0.1 eq.66
  68.8 182.8 %all-to-all-done.1 = bf16[16,16,16384]{2,1,0:T(8,128)(2,1)} async-done(((bf16[16,16,16384]{2,1,0:T(8,128)(2,1)}), bf16[16,16,16384]{2,1,0:T(8,128)(2,1)}, u32[]{:S(2)}, u32[]{:S(2)}) %all-to-all-start.1) | async-done | bytes 8388640 | tf_op jit(solution)/shard_map/all_to_all | solution.py:82
  251.6 12.0 %fusion.17 = (bf16[256,16384]{1,0:T(8,128)(2,1)S(1)}, f32[256,16384]{1,0:T(8,128)}) fusion(bf16[256,16384]{1,0:T(8,128)(2,1)} %bitcast.7, s32[256]{0:T(256)S(1)} %eq.66), kind=kOutput, calls=%fused_computation.57 | convolution fusion | flops 2151743488 | bytes 33555456 | tf_op jit(solution)/shard_map/dot_general | solution.py:34
  263.6 0.3 select_bitcast_fusion
  263.9 0.1 copy.41
  264.0 1.2 copy.29
  265.1 0.1 copy.35
  265.2 1.2 copy.23
  266.4 0.1 copy.36
  266.5 1.1 copy.24
  267.6 0.1 copy.39
  267.7 1.1 copy.27
  268.9 0.1 copy.40
  269.0 1.1 copy.28
  270.1 0.1 copy.38
  270.2 1.2 copy.26
  271.3 0.1 copy.34
  271.4 1.2 copy.22
  272.6 0.1 copy.37
  272.7 1.1 copy.25
  273.8 0.0 all-reduce.3.cloned.1.call-update
  273.9 0.3 all-gather.2.cloned.1.call-start
  274.1 0.3 all-gather.2.cloned.1.call-update
  274.4 14.3 %copy.33 = f32[32,8,128,128]{3,2,1,0:T(8,128)} copy(f32[32,8,128,128]{3,1,2,0:T(8,128)} %bitcast.72) | data formatting | bytes 33554432
  288.8 70.7 %all-reduce.3.cloned.1.call-done = (bf16[1,16,128,128]{3,1,2,0:T(8,128)(2,1)}, bf16[1,16,128,128]{3,1,2,0:T(8,128)(2,1)}, bf16[1,16,128,128]{3,1,2,0:T(8,128)(2,...) async-done(((bf16[1,16,128,128]{3,1,2,0:T(8,128)(2,1)}, ...) | async-done | bytes 4194320 | tf_op jit(solution)/shard_map/psum | solution.py:12
  359.5 0.0 copy-start.2
  359.5 0.0 copy-start.1
  359.5 0.0 copy-start
  359.5 2.0 constant_dynamic-update-slice_fusion.7
  361.5 1.9 constant_dynamic-update-slice_fusion.6
  363.3 1.9 constant_dynamic-update-slice_fusion.5
  365.2 1.9 constant_dynamic-update-slice_fusion.4
  367.1 1.9 constant_dynamic-update-slice_fusion.3
  368.9 0.0 copy-done.2
  368.9 0.8 constant_dynamic-update-slice_fusion.2
  369.8 0.0 copy-done.1
  369.8 0.8 constant_dynamic-update-slice_fusion.1
  370.6 0.0 copy-done
  370.6 0.8 constant_dynamic-update-slice_fusion
  371.4 0.0 all-gather.2.cloned.1.call-done
  371.4 12.6 %convolution_bitcast_fusion = f32[256,8,16,128]{3,1,2,0:T(8,128)S(1)} fusion(bf16[2048,1024]{1,0:T(8,128)(2,1)} %bitcast.88, bf16[128,8,16,128]{3,2,1,0:T(8,128)(2,1)} %bitcast.44), kind=kOutput, calls=%fused_computation.2 | convolution fusion | flops 8589934592 | bytes 25165824 | tf_op jit(solution)/shard_map/dot_general | solution.py:100
  384.0 7.5 %copy.43 = f32[256,8,16,128]{3,2,1,0:T(8,128)} copy(f32[256,8,16,128]{3,1,2,0:T(8,128)S(1)} %convolution_bitcast_fusion) | data formatting | bytes 33554432
  391.5 24.9 %copy.31 = f32[16,1,128,16,1,128]{5,4,3,2,1,0:T(1,128)} copy(f32[16,1,128,16,1,128]{2,0,5,3,4,1:T(8,128)} %bitcast.73) | data formatting | bytes 33554432
  (3 shorter events, 0.0 us)
Async XLA Ops:
  10.6 50.6 %all-to-all-start = ((s32[16,1,16]{2,1,0:T(1,128)}), s32[16,1,16]{2,1,0:T(1,128)S(1)}, u32[]{:S(2)}, u32[]{:S(2)}) async-start(s32[16,1,16]{2,1,0:T(1,128)} %sub.19), calls=%async_computation | async-start | bytes 16384 | tf_op jit(solution)/shard_map/all_to_all | solution.py:83
  61.2 190.4 %all-to-all-start.1 = ((bf16[16,16,16384]{2,1,0:T(8,128)(2,1)}), bf16[16,16,16384]{2,1,0:T(8,128)(2,1)}, u32[]{:S(2)}, u32[]{:S(2)}) async-start(bf16[16,16,16384]{2,1,0:T(8,128)(2,1)} %bitcast.74), calls=%async_computation.1 | async-start | bytes 16777216 | tf_op jit(solution)/shard_map/all_to_all | solution.py:82
  67.3 292.2 %all-reduce.3.cloned.1.call-start = ((), (), s32[]{:S(2)}) async-start(), calls=%async_computation.3 | async-start | bytes 8388608 | tf_op jit(solution)/shard_map/psum | solution.py:12
  273.9 97.6 %all-gather.2.cloned.1.call-start = ((), (), s32[]{:S(2)}) async-start(), calls=%async_computation.2 | async-start | bytes 5242880 | tf_op jit(solution)/shard_map/all_gather | solution.py:98
  359.5 9.5 %copy-start.2 = (bf16[1,16,128,128]{3,1,2,0:T(8,128)(2,1)S(1)}, bf16[1,16,128,128]{3,1,2,0:T(8,128)(2,1)}, u32[]{:S(2)}) copy-start(bf16[1,16,128,128]{3,1,2,0:T(8,128)(2,1)} %get-tuple-element.13) | copy-start | bytes 1572868
  359.5 10.3 %copy-start.1 = (bf16[1,16,128,128]{3,1,2,0:T(8,128)(2,1)S(1)}, bf16[1,16,128,128]{3,1,2,0:T(8,128)(2,1)}, u32[]{:S(2)}) copy-start(bf16[1,16,128,128]{3,1,2,0:T(8,128)(2,1)} %get-tuple-element.14) | copy-start | bytes 1572868
  359.5 11.1 %copy-start = (bf16[1,16,128,128]{3,1,2,0:T(8,128)(2,1)S(1)}, bf16[1,16,128,128]{3,1,2,0:T(8,128)(2,1)}, u32[]{:S(2)}) copy-start(bf16[1,16,128,128]{3,1,2,0:T(8,128)(2,1)} %get-tuple-element.15) | copy-start | bytes 1572868
Sparse Core Ops, SparseCore 0:
  274.0 85.4 all-reduce.2
Sparse Core Ops, SparseCore 1:
  275.9 79.1 all-gather.1
where the time goes:
time: 425 us; the launch traced here: 424 us
  waiting for transfers between devices  254 us (60%)
  local copies, waits for them, and re-layouts  91.6 us (22%)
  matrix products  47.6 us (11%)
  between operations  15.6 us (4%)
  starting transfers between devices  13.9 us (3%)
    all_to_all x1, waiting for transfers between devices, local(): lax.all_to_all(packed, ('row', 'col'), split_axis=0, concat_axis=0, tiled...  183 us
    psum x1, waiting for transfers between devices, from_root(): return lax.psum(kept, axis)  70.7 us
    unnamed x24, local copies, waits for them, and re-layouts  58.6 us
    dot_general x1, matrix products, local(): lax.dot_general(phi_batch, weighted, (((0,), (0,)), ((), ())), preferred_...  15.6 us
    dot_general x1, matrix products, local(): jnp.dot(piece.reshape(local_rows * block_size, width), head_matrix, prefe...  12.6 us
    dot_general x1, matrix products, sum_into_tile(): lax.dot_general(selector.astype(jnp.bfloat16), received, (((0,), (0,)), (...  12 us
    another operation x9, local copies, waits for them, and re-layouts, local(): head_stack = jnp.stack(gathered_rows, axis=0)  10 us
    reshape x1, local copies, waits for them, and re-layouts, local(): partial_sum.reshape(list_length, block_size, list_length, block_size)  9.42 us
  transfers between devices with their start and end apart: 4, of which 2 were waited for; matrix products, arithmetic and copies ran while one was open for 17% of the time, Pallas kernels for 0%

commit v1 on v0

--- a/solution.py
+++ b/solution.py
@@ -5,6 +5,29 @@
 
 NB = 8192
 WIN = 16
+
+
+def in_blocks(array, dim, size):
+    shape = array.shape
+    tiles = array.reshape(*shape[:dim], size, shape[dim] // size, *shape[dim + 1 :])
+    return jnp.moveaxis(tiles, dim, 0)
+
+
+def joined_along(blocks, dim):
+    dims = list(blocks.shape[1:])
+    dims[dim] *= blocks.shape[0]
+    return jnp.moveaxis(blocks, 0, dim).reshape(dims)
+
+
+def swapped_with_each(value, axis, split_dim, concat_dim):
+    size, index = (lax.axis_size(axis), lax.axis_index(axis))
+    blocks = in_blocks(value, split_dim, size)
+    done = [blocks[index]]
+    for turn in range(1, size):
+        sent = blocks[index ^ turn]
+        done.append(lax.ppermute(sent, axis, [(i, i ^ turn) for i in range(size)]))
+    blocks = jnp.stack(done)[index ^ jnp.arange(size)]
+    return joined_along(blocks, concat_dim)
 
 
 def from_root(value, axis, source):
@@ -79,7 +102,7 @@
     packed = packed.reshape(device_count, capacity, block_area)
     slot_labels = slot_labels.reshape(device_count, capacity)
     received, received_labels = (
-        lax.all_to_all(packed, ("row", "col"), split_axis=0, concat_axis=0, tiled=True),
+        swapped_with_each(packed, ("row", "col"), 0, 0),
         lax.all_to_all(slot_labels, ("row", "col"), split_axis=0, concat_axis=0, tiled=True),
     )
     tile = sum_into_tile(received.reshape(-1, block_area), received_labels.reshape(-1), tile_blocks)

time: 425 us -> 501 us (1.18)
  starting transfers between devices: 13.9 us -> 45.1 us
  local copies, waits for them, and re-layouts: 91.6 us -> 121 us
  waiting for transfers between devices: 254 us -> 270 us
    ppermute x0 -> x15, waiting for transfers between devices: none -> 187 us  [swapped_with_each(): done.append(lax.ppermute(sent, axis, [(i, i ^ turn) for i in range(size)]))]
    all_to_all x1 -> x0, waiting for transfers between devices: 183 us -> none  [local(): lax.all_to_all(packed, ('row', 'col'), split_axis=0, concat_axis=0, tiled...]
    ppermute x0 -> x15, starting transfers between devices: none -> 39.8 us  [swapped_with_each(): done.append(lax.ppermute(sent, axis, [(i, i ^ turn) for i in range(size)]))]
    unnamed x24 -> x36, local copies, waits for them, and re-layouts: 58.6 us -> 71.9 us
    gather x0 -> x1, local copies, waits for them, and re-layouts: none -> 8.31 us  [swapped_with_each(): blocks = jnp.stack(done)[index ^ jnp.arange(size)]]
    psum x1, waiting for transfers between devices: 70.7 us -> 78.3 us  [from_root(): return lax.psum(kept, axis)]
    all_to_all x1 -> x0, starting transfers between devices: 6.06 us -> none  [local(): lax.all_to_all(packed, ('row', 'col'), split_axis=0, concat_axis=0, tiled...]
  transfers between devices with their start and end apart: 4 -> 18, of which waited for: 2 -> 12; matrix products, arithmetic and copies ran while one was open for 17% -> 9% of each run, Pallas kernels for 0% -> 0%
where the time goes in v1:
time: 501 us; the launch traced here: 499 us
  waiting for transfers between devices  270 us (54%)
  local copies, waits for them, and re-layouts  121 us (24%)
  matrix products  46.5 us (9%)
  starting transfers between devices  45.1 us (9%)
  between operations  15.7 us (3%)
    ppermute x15, waiting for transfers between devices, swapped_with_each(): done.append(lax.ppermute(sent, axis, [(i, i ^ turn) for i in range(size)]))  187 us
    psum x1, waiting for transfers between devices, from_root(): return lax.psum(kept, axis)  78.3 us
    unnamed x36, local copies, waits for them, and re-layouts  71.9 us
    ppermute x15, starting transfers between devices, swapped_with_each(): done.append(lax.ppermute(sent, axis, [(i, i ^ turn) for i in range(size)]))  39.8 us
    dot_general x1, matrix products, local(): lax.dot_general(phi_batch, weighted, (((0,), (0,)), ((), ())), preferred_...  15.6 us
    dot_general x1, matrix products, local(): jnp.dot(piece.reshape(local_rows * block_size, width), head_matrix, prefe...  12.6 us
    dot_general x1, matrix products, sum_into_tile(): lax.dot_general(selector.astype(jnp.bfloat16), received, (((0,), (0,)), (...  12 us
    another operation x9, local copies, waits for them, and re-layouts, local(): head_stack = jnp.stack(gathered_rows, axis=0)  11.1 us
  transfers between devices with their start and end apart: 18, of which 12 were waited for; matrix products, arithmetic and copies ran while one was open for 9% of the time, Pallas kernels for 0%

profile of v1, /device:TPU:0, one launch (start us, length us, event | category | flops | bytes accessed | tf_op | source)
XLA Modules:
  0.0 499.2 jit_solution(15266270771601949047)
XLA Ops:
  9.9 15.6 %fusion = bf16[1536,1536]{0,1:T(8,128)(2,1)} fusion(bf16[1,1,2048,1536]{3,2,1,0:T(8,128)(2,1)} %param.4, f32[2048]{0:T(1024)} %bitcast.154), kind=kOutput, calls=%fused_computation.5 | convolution fusion | flops 9675472896 | bytes 11018240 | tf_op jit(solution)/shard_map/dot_general | solution.py:81
  25.5 6.6 %copy.20 = bf16[1536,1536]{1,0:T(8,128)(2,1)} copy(bf16[1536,1536]{0,1:T(8,128)(2,1)} %fusion) | data formatting | bytes 9437184 | tf_op jit(solution)/shard_map/convert_element_type | solution.py:83
  32.1 9.4 %reshape.297 = bf16[12,128,12,128]{3,2,1,0:T(8,128)(2,1)} reshape(bf16[1536,1536]{1,0:T(8,128)(2,1)} %copy.20) | data formatting | bytes 9437184 | tf_op jit(solution)/shard_map/reshape | solution.py:84
  41.5 6.3 %copy.21 = bf16[12,12,128,128]{3,2,1,0:T(8,128)(2,1)} copy(bf16[12,12,128,128]{3,1,2,0:T(8,128)(2,1)} %bitcast.139) | data formatting | bytes 9437184 | tf_op jit(solution)/shard_map/transpose | solution.py:84
  47.8 6.3 %convolution_convert_fusion = bf16[256,16384]{1,0:T(8,128)(2,1)S(1)} fusion(bf16[18,8,128,128]{3,2,1,0:T(8,128)(2,1)} %bitcast.140, s32[144]{0:T(256)S(1)} %multiply_add_fusion), kind=kOutput, calls=%fused_computation.1 | convolution fusion | flops 1212190720 | bytes 13107776 | tf_op jit(solution)/shard_map/dot_general | solution.py:48
  54.1 3.2 dynamic-slice_bitcast_fusion
  57.4 3.0 collective-permute-start
  61.2 4.9 all-to-all-start
  66.3 4.4 collective-permute-start.14
  70.8 1.8 collective-permute-start.12
  72.6 4.5 all-to-all-done
  78.9 0.8 bitcast_dynamic-update-slice_fusion.14
  79.7 67.3 %collective-permute-done.1 = bf16[1,16,16384]{2,1,0:T(8,128)(2,1)S(1)} collective-permute-done((bf16[1,16,16384]{2,1,0:T(8,128)(2,1)}, bf16[1,16,16384]{2,1,0:T(8,128)(2,1)S(1)}, u32[]{:S(2)}, u32[]{:S(2)}) %collective-permute-start.1) | collective-permute-done | bytes 524320 | tf_op jit(solution)/shard_map/ppermute | solution.py:28
  147.0 2.8 collective-permute-start.2
  149.8 0.8 bitcast_dynamic-update-slice_fusion.13
  150.6 12.1 %collective-permute-done.2 = bf16[1,16,16384]{2,1,0:T(8,128)(2,1)S(1)} collective-permute-done((bf16[1,16,16384]{2,1,0:T(8,128)(2,1)}, bf16[1,16,16384]{2,1,0:T(8,128)(2,1)S(1)}, u32[]{:S(2)}, u32[]{:S(2)}) %collective-permute-start.2) | collective-permute-done | bytes 524320 | tf_op jit(solution)/shard_map/ppermute | solution.py:28
  162.8 0.8 bitcast_dynamic-update-slice_fusion.12
  163.6 1.3 collective-permute-done.3
  164.9 9.1 %collective-permute-start.4 = (bf16[1,16,16384]{2,1,0:T(8,128)(2,1)}, bf16[1,16,16384]{2,1,0:T(8,128)(2,1)S(1)}, u32[]{:S(2)}, u32[]{:S(2)}) collective-permute-start(bf16[1,16,16384]{2,1,0:T(8,128)(2,1)} %get-tuple-element.34), channel_id=1, source_target_pairs={{0,5},{1,4},{2,7},{3,6},{4,1},{5,0},{6,3},{7,2},{8,13},{9,12},{10,... | collective-permute-start | bytes 1572872 | tf_op jit(solution)/shard_map/ppermute | solution.py:28
  174.0 0.8 bitcast_dynamic-update-slice_fusion.11
  174.9 11.5 %collective-permute-done.4 = bf16[1,16,16384]{2,1,0:T(8,128)(2,1)S(1)} collective-permute-done((bf16[1,16,16384]{2,1,0:T(8,128)(2,1)}, bf16[1,16,16384]{2,1,0:T(8,128)(2,1)S(1)}, u32[]{:S(2)}, u32[]{:S(2)}) %collective-permute-start.4) | collective-permute-done | bytes 524320 | tf_op jit(solution)/shard_map/ppermute | solution.py:28
  186.3 1.5 collective-permute-start.5
  187.9 0.8 bitcast_dynamic-update-slice_fusion.10
  188.7 23.9 %collective-permute-done.5 = bf16[1,16,16384]{2,1,0:T(8,128)(2,1)S(1)} collective-permute-done((bf16[1,16,16384]{2,1,0:T(8,128)(2,1)}, bf16[1,16,16384]{2,1,0:T(8,128)(2,1)S(1)}, u32[]{:S(2)}, u32[]{:S(2)}) %collective-permute-start.5) | collective-permute-done | bytes 524320 | tf_op jit(solution)/shard_map/ppermute | solution.py:28
  212.6 1.2 collective-permute-start.6
  213.9 0.8 bitcast_dynamic-update-slice_fusion.9
  214.7 14.0 %collective-permute-done.6 = bf16[1,16,16384]{2,1,0:T(8,128)(2,1)S(1)} collective-permute-done((bf16[1,16,16384]{2,1,0:T(8,128)(2,1)}, bf16[1,16,16384]{2,1,0:T(8,128)(2,1)S(1)}, u32[]{:S(2)}, u32[]{:S(2)}) %collective-permute-start.6) | collective-permute-done | bytes 524320 | tf_op jit(solution)/shard_map/ppermute | solution.py:28
  228.7 0.8 bitcast_dynamic-update-slice_fusion.8
  229.5 13.3 %collective-permute-done.7 = bf16[1,16,16384]{2,1,0:T(8,128)(2,1)S(1)} collective-permute-done((bf16[1,16,16384]{2,1,0:T(8,128)(2,1)}, bf16[1,16,16384]{2,1,0:T(8,128)(2,1)S(1)}, u32[]{:S(2)}, u32[]{:S(2)}) %collective-permute-start.7) | collective-permute-done | bytes 524320 | tf_op jit(solution)/shard_map/ppermute | solution.py:28
  242.8 8.4 %collective-permute-start.8 = (bf16[1,16,16384]{2,1,0:T(8,128)(2,1)}, bf16[1,16,16384]{2,1,0:T(8,128)(2,1)S(1)}, u32[]{:S(2)}, u32[]{:S(2)}) collective-permute-start(bf16[1,16,16384]{2,1,0:T(8,128)(2,1)} %get-tuple-element.30), channel_id=1, source_target_pairs={{0,9},{1,8},{2,11},{3,10},{4,13},{5,12},{6,15},{7,14},{8,1},{9,0},... | collective-permute-start | bytes 1572872 | tf_op jit(solution)/shard_map/ppermute | solution.py:28
  251.2 0.8 bitcast_dynamic-update-slice_fusion.7
  252.0 11.0 %collective-permute-done.8 = bf16[1,16,16384]{2,1,0:T(8,128)(2,1)S(1)} collective-permute-done((bf16[1,16,16384]{2,1,0:T(8,128)(2,1)}, bf16[1,16,16384]{2,1,0:T(8,128)(2,1)S(1)}, u32[]{:S(2)}, u32[]{:S(2)}) %collective-permute-start.8) | collective-permute-done | bytes 524320 | tf_op jit(solution)/shard_map/ppermute | solution.py:28
  263.0 3.6 collective-permute-start.9
  267.5 21.4 %collective-permute-done.9 = bf16[1,16,16384]{2,1,0:T(8,128)(2,1)S(1)} collective-permute-done((bf16[1,16,16384]{2,1,0:T(8,128)(2,1)S(1)}, bf16[1,16,16384]{2,1,0:T(8,128)(2,1)S(1)}, u32[]{:S(2)}, u32[]{:S(2)}) %collective-permute-start.9) | collective-permute-done | bytes 524320 | tf_op jit(solution)/shard_map/ppermute | solution.py:28
  288.8 3.4 collective-permute-start.10
  293.1 10.9 %collective-permute-done.10 = bf16[1,16,16384]{2,1,0:T(8,128)(2,1)S(1)} collective-permute-done((bf16[1,16,16384]{2,1,0:T(8,128)(2,1)S(1)}, bf16[1,16,16384]{2,1,0:T(8,128)(2,1)S(1)}, u32[]{:S(2)}, u32[]{:S(2)}) %collective-permute-start.10) | collective-permute-done | bytes 524320 | tf_op jit(solution)/shard_map/ppermute | solution.py:28
  304.0 0.8 bitcast_dynamic-update-slice_fusion.4
  304.9 0.8 bitcast_dynamic-update-slice_fusion.3
  305.7 0.8 bitcast_dynamic-update-slice_fusion.2
  306.5 0.8 bitcast_dynamic-update-slice_fusion.1
  307.3 0.8 bitcast_dynamic-update-slice_fusion
  308.2 8.3 %gather_fusion = bf16[16,16,16384]{2,1,0:T(8,128)(2,1)} fusion(bf16[16,16,16384]{2,1,0:T(8,128)(2,1)} %bitcast.142, s32[1024]{0:T(1024)S(1)} %pad_clamp_fusion), kind=kCustom, calls=%fused_computation | custom fusion | bytes 16777280 | tf_op jit(solution)/shard_map/gather | solution.py:29
  316.5 12.0 %fusion.18 = (bf16[256,16384]{1,0:T(8,128)(2,1)S(1)}, f32[256,16384]{1,0:T(8,128)}) fusion(bf16[256,16384]{1,0:T(8,128)(2,1)} %bitcast.138, s32[256]{0:T(256)S(1)} %eq.66), kind=kOutput, calls=%fused_computation.92 | convolution fusion | flops 2151743488 | bytes 33555456 | tf_op jit(solution)/shard_map/dot_general | solution.py:57
  328.9 1.1 copy.29
  330.1 1.2 copy.23
  331.4 1.1 copy.24
  332.6 1.1 copy.27
  333.8 1.1 copy.28
  335.1 1.1 copy.26
  336.3 1.2 copy.22
  337.6 1.2 copy.25
  339.3 14.2 %copy.33 = f32[32,8,128,128]{3,2,1,0:T(8,128)} copy(f32[32,8,128,128]{3,1,2,0:T(8,128)} %bitcast.135) | data formatting | bytes 33554432
  353.5 78.3 %all-reduce.3.cloned.1.call-done = (bf16[1,16,128,128]{3,1,2,0:T(8,128)(2,1)}, bf16[1,16,128,128]{3,1,2,0:T(8,128)(2,1)}, bf16[1,16,128,128]{3,1,2,0:T(8,128)(2,...) async-done(((bf16[1,16,128,128]{3,1,2,0:T(8,128)(2,1)}, ...) | async-done | bytes 4194320 | tf_op jit(solution)/shard_map/psum | solution.py:35
  431.8 1.9 constant_dynamic-update-slice_fusion.7
  433.7 1.9 constant_dynamic-update-slice_fusion.6
  435.6 1.9 constant_dynamic-update-slice_fusion.5
  437.4 1.9 constant_dynamic-update-slice_fusion.4
  439.3 1.9 constant_dynamic-update-slice_fusion.3
  441.2 1.9 constant_dynamic-update-slice_fusion.2
  443.0 1.9 constant_dynamic-update-slice_fusion.1
  444.9 1.9 constant_dynamic-update-slice_fusion
  446.8 12.6 %convolution_bitcast_fusion = f32[256,8,16,128]{3,1,2,0:T(8,128)S(1)} fusion(bf16[2048,1024]{1,0:T(8,128)(2,1)} %bitcast.153, bf16[128,8,16,128]{3,2,1,0:T(8,128)(2,1)} %bitcast.76), kind=kOutput, calls=%fused_computation.3 | convolution fusion | flops 8589934592 | bytes 25165824 | tf_op jit(solution)/shard_map/dot_general | solution.py:123
  459.4 7.5 %copy.43 = f32[256,8,16,128]{3,2,1,0:T(8,128)} copy(f32[256,8,16,128]{3,1,2,0:T(8,128)S(1)} %convolution_bitcast_fusion) | data formatting | bytes 33554432
  466.9 24.9 %copy.31 = f32[16,1,128,16,1,128]{5,4,3,2,1,0:T(1,128)} copy(f32[16,1,128,16,1,128]{2,0,5,3,4,1:T(8,128)} %bitcast.136) | data formatting | bytes 33554432
  (45 shorter events, 7.9 us)
Async XLA Ops:
  57.4 21.2 %collective-permute-start = (bf16[1,16,16384]{2,1,0:T(8,128)(2,1)}, bf16[1,16,16384]{2,1,0:T(8,128)(2,1)S(1)}, u32[]{:S(2)}, u32[]{:S(2)}) collective-permute-start(bf16[1,16,16384]{2,1,0:T(8,128)(2,1)} %get-tuple-element.38), channel_id=1, source_target_pairs={{0,1},{1,0},{2,3},{3,2},{4,5},{5,4},{6,7},{7,6},{8,9},{9,8},{10,11... | collective-permute-start | bytes 1572872 | tf_op jit(solution)/shard_map/ppermute | solution.py:28
  61.2 15.9 %all-to-all-start = ((s32[16,1,16]{2,1,0:T(1,128)}), s32[16,1,16]{2,1,0:T(1,128)S(1)}, u32[]{:S(2)}, u32[]{:S(2)}) async-start(s32[16,1,16]{2,1,0:T(1,128)} %sub.19), calls=%async_computation | async-start | bytes 16384 | tf_op jit(solution)/shard_map/all_to_all | solution.py:106
  66.1 365.7 %all-reduce.3.cloned.1.call-start = ((), (), s32[]{:S(2)}) async-start(), calls=%async_computation.2 | async-start | bytes 8388608 | tf_op jit(solution)/shard_map/psum | solution.py:35
  66.3 241.0 %collective-permute-start.14 = (bf16[1,16,16384]{2,1,0:T(8,128)(2,1)S(1)}, bf16[1,16,16384]{2,1,0:T(8,128)(2,1)S(1)}, u32[]{:S(2)}, u32[]{:S(2)}) collective-permute-start(bf16[1,16,16384]{2,1,0:T(8,128)(2,1)S(1)} %get-tuple-element.24), channel_id=1, source_target_pairs={{0,15},{1,14},{2,13},{3,12},{4,11},{5,10},{6,9},{7,8},{8,7},{9,6},... | collective-permute-start | bytes 1572872 | tf_op jit(solution)/shard_map/ppermute | solution.py:28
  70.8 235.7 %collective-permute-start.13 = (bf16[1,16,16384]{2,1,0:T(8,128)(2,1)}, bf16[1,16,16384]{2,1,0:T(8,128)(2,1)S(1)}, u32[]{:S(2)}, u32[]{:S(2)}) collective-permute-start(bf16[1,16,16384]{2,1,0:T(8,128)(2,1)} %get-tuple-element.25), channel_id=1, source_target_pairs={{0,14},{1,15},{2,12},{3,13},{4,10},{5,11},{6,8},{7,9},{8,6},{9,7},... | collective-permute-start | bytes 1572872 | tf_op jit(solution)/shard_map/ppermute | solution.py:28
  70.8 234.9 %collective-permute-start.12 = (bf16[1,16,16384]{2,1,0:T(8,128)(2,1)}, bf16[1,16,16384]{2,1,0:T(8,128)(2,1)S(1)}, u32[]{:S(2)}, u32[]{:S(2)}) collective-permute-start(bf16[1,16,16384]{2,1,0:T(8,128)(2,1)} %get-tuple-element.26), channel_id=1, source_target_pairs={{0,13},{1,12},{2,15},{3,14},{4,9},{5,8},{6,11},{7,10},{8,5},{9,4},... | collective-permute-start | bytes 1572872 | tf_op jit(solution)/shard_map/ppermute | solution.py:28
  72.5 232.3 %collective-permute-start.11 = (bf16[1,16,16384]{2,1,0:T(8,128)(2,1)}, bf16[1,16,16384]{2,1,0:T(8,128)(2,1)S(1)}, u32[]{:S(2)}, u32[]{:S(2)}) collective-permute-start(bf16[1,16,16384]{2,1,0:T(8,128)(2,1)} %get-tuple-element.27), channel_id=1, source_target_pairs={{0,12},{1,13},{2,14},{3,15},{4,8},{5,9},{6,10},{7,11},{8,4},{9,5},... | collective-permute-start | bytes 1572872 | tf_op jit(solution)/shard_map/ppermute | solution.py:28
  78.5 184.5 %copy-start.1 = (bf16[1,16,16384]{2,1,0:T(8,128)(2,1)S(1)}, bf16[1,16,16384]{2,1,0:T(8,128)(2,1)}, u32[]{:S(2)}) copy-start(bf16[1,16,16384]{2,1,0:T(8,128)(2,1)} %get-tuple-element.29) | copy-start | bytes 1572868
  78.5 210.3 %copy-start = (bf16[1,16,16384]{2,1,0:T(8,128)(2,1)S(1)}, bf16[1,16,16384]{2,1,0:T(8,128)(2,1)}, u32[]{:S(2)}) copy-start(bf16[1,16,16384]{2,1,0:T(8,128)(2,1)} %get-tuple-element.28) | copy-start | bytes 1572868
  78.5 68.5 %collective-permute-start.1 = (bf16[1,16,16384]{2,1,0:T(8,128)(2,1)}, bf16[1,16,16384]{2,1,0:T(8,128)(2,1)S(1)}, u32[]{:S(2)}, u32[]{:S(2)}) collective-permute-start(bf16[1,16,16384]{2,1,0:T(8,128)(2,1)} %get-tuple-element.37), channel_id=1, source_target_pairs={{0,2},{1,3},{2,0},{3,1},{4,6},{5,7},{6,4},{7,5},{8,10},{9,11},{10,... | collective-permute-start | bytes 1572872 | tf_op jit(solution)/shard_map/ppermute | solution.py:28
  147.0 15.7 %collective-permute-start.2 = (bf16[1,16,16384]{2,1,0:T(8,128)(2,1)}, bf16[1,16,16384]{2,1,0:T(8,128)(2,1)S(1)}, u32[]{:S(2)}, u32[]{:S(2)}) collective-permute-start(bf16[1,16,16384]{2,1,0:T(8,128)(2,1)} %get-tuple-element.36), channel_id=1, source_target_pairs={{0,3},{1,2},{2,1},{3,0},{4,7},{5,6},{6,5},{7,4},{8,11},{9,10},{10,... | collective-permute-start | bytes 1572872 | tf_op jit(solution)/shard_map/ppermute | solution.py:28
  162.8 2.1 collective-permute-start.3
  164.9 21.4 %collective-permute-start.4 = (bf16[1,16,16384]{2,1,0:T(8,128)(2,1)}, bf16[1,16,16384]{2,1,0:T(8,128)(2,1)S(1)}, u32[]{:S(2)}, u32[]{:S(2)}) collective-permute-start(bf16[1,16,16384]{2,1,0:T(8,128)(2,1)} %get-tuple-element.34), channel_id=1, source_target_pairs={{0,5},{1,4},{2,7},{3,6},{4,1},{5,0},{6,3},{7,2},{8,13},{9,12},{10,... | collective-permute-start | bytes 1572872 | tf_op jit(solution)/shard_map/ppermute | solution.py:28
  186.3 26.3 %collective-permute-start.5 = (bf16[1,16,16384]{2,1,0:T(8,128)(2,1)}, bf16[1,16,16384]{2,1,0:T(8,128)(2,1)S(1)}, u32[]{:S(2)}, u32[]{:S(2)}) collective-permute-start(bf16[1,16,16384]{2,1,0:T(8,128)(2,1)} %get-tuple-element.33), channel_id=1, source_target_pairs={{0,6},{1,7},{2,4},{3,5},{4,2},{5,3},{6,0},{7,1},{8,14},{9,15},{10,... | collective-permute-start | bytes 1572872 | tf_op jit(solution)/shard_map/ppermute | solution.py:28
  212.6 16.0 %collective-permute-start.6 = (bf16[1,16,16384]{2,1,0:T(8,128)(2,1)}, bf16[1,16,16384]{2,1,0:T(8,128)(2,1)S(1)}, u32[]{:S(2)}, u32[]{:S(2)}) collective-permute-start(bf16[1,16,16384]{2,1,0:T(8,128)(2,1)} %get-tuple-element.32), channel_id=1, source_target_pairs={{0,7},{1,6},{2,5},{3,4},{4,3},{5,2},{6,1},{7,0},{8,15},{9,14},{10,... | collective-permute-start | bytes 1572872 | tf_op jit(solution)/shard_map/ppermute | solution.py:28
  228.7 14.2 %collective-permute-start.7 = (bf16[1,16,16384]{2,1,0:T(8,128)(2,1)}, bf16[1,16,16384]{2,1,0:T(8,128)(2,1)S(1)}, u32[]{:S(2)}, u32[]{:S(2)}) collective-permute-start(bf16[1,16,16384]{2,1,0:T(8,128)(2,1)} %get-tuple-element.31), channel_id=1, source_target_pairs={{0,8},{1,9},{2,10},{3,11},{4,12},{5,13},{6,14},{7,15},{8,0},{9,1},... | collective-permute-start | bytes 1572872 | tf_op jit(solution)/shard_map/ppermute | solution.py:28
  242.8 20.2 %collective-permute-start.8 = (bf16[1,16,16384]{2,1,0:T(8,128)(2,1)}, bf16[1,16,16384]{2,1,0:T(8,128)(2,1)S(1)}, u32[]{:S(2)}, u32[]{:S(2)}) collective-permute-start(bf16[1,16,16384]{2,1,0:T(8,128)(2,1)} %get-tuple-element.30), channel_id=1, source_target_pairs={{0,9},{1,8},{2,11},{3,10},{4,13},{5,12},{6,15},{7,14},{8,1},{9,0},... | collective-permute-start | bytes 1572872 | tf_op jit(solution)/shard_map/ppermute | solution.py:28
  263.0 25.8 %collective-permute-start.9 = (bf16[1,16,16384]{2,1,0:T(8,128)(2,1)S(1)}, bf16[1,16,16384]{2,1,0:T(8,128)(2,1)S(1)}, u32[]{:S(2)}, u32[]{:S(2)}) collective-permute-start(bf16[1,16,16384]{2,1,0:T(8,128)(2,1)S(1)} %copy-done.1), channel_id=1, source_target_pairs={{0,10},{1,11},{2,8},{3,9},{4,14},{5,15},{6,12},{7,13},{8,2},{9,3},... | collective-permute-start | bytes 1572872 | tf_op jit(solution)/shard_map/ppermute | solution.py:28
  288.8 15.2 %collective-permute-start.10 = (bf16[1,16,16384]{2,1,0:T(8,128)(2,1)S(1)}, bf16[1,16,16384]{2,1,0:T(8,128)(2,1)S(1)}, u32[]{:S(2)}, u32[]{:S(2)}) collective-permute-start(bf16[1,16,16384]{2,1,0:T(8,128)(2,1)S(1)} %copy-done), channel_id=1, source_target_pairs={{0,11},{1,10},{2,9},{3,8},{4,15},{5,14},{6,13},{7,12},{8,3},{9,2},... | collective-permute-start | bytes 1572872 | tf_op jit(solution)/shard_map/ppermute | solution.py:28
  338.8 108.0 %all-gather.2.cloned.1.call-start = ((), (), s32[]{:S(2)}) async-start(), calls=%async_computation.1 | async-start | bytes 5242880 | tf_op jit(solution)/shard_map/all_gather | solution.py:121
Sparse Core Ops, SparseCore 0:
  338.9 92.9 all-reduce.2
Sparse Core Ops, SparseCore 1:
  340.8 86.5 all-gather.1
